TPU v7x, 32 devices: a whole 2x2x4 slice. The times are simulated.
32 devices in a mesh: gx: 8 (over z, y), gy: 4 (over x, core).
Axes of the slice: x: 2, y: 2, z: 4, core: 2. Of those that a mesh axis runs over, the one named last changes fastest.
Arguments:
- force: float32 [32, 1024, 1024], P(None, 'gx', 'gy'), may hold values from -6 to 6
- drag: float32 [32], replicated, may hold values from 0.5 to 2
Outputs:
- velocity: float32 [32, 1024, 1024], P(None, 'gx', 'gy')
All inputs are finite; a program needn't handle non-finite values.
Results may differ from a plain program's by a relative error of at most 0.0003.
Values sent between devices are 32-bit elements; how exact they have to be, the bound alone decides.
A program may use at most 192 MiB of HBM per device.

v0:
```python
import math

import jax
import jax.numpy as jnp
from jax import lax
from jax.sharding import PartitionSpec as P

HIGH = lax.Precision.HIGHEST


def tables(row_pos, col_pos, length):
    phase = row_pos[:, None] * col_pos[None, :] % length
    angle = phase.astype(jnp.float32) * (2.0 * math.pi / length)
    return (jnp.cos(angle), jnp.sin(angle))


def green_block(drag, x_pos, y_pos, len_x, len_y):
    mode_x = jnp.where(x_pos < len_x // 2, x_pos, x_pos - len_x).astype(jnp.float32)
    mode_y = jnp.where(y_pos < len_y // 2, y_pos, y_pos - len_y).astype(jnp.float32)
    square = mode_x[:, None] ** 2 + mode_y[None, :] ** 2
    project = 1.0 - mode_x[:, None] ** 2 / jnp.maximum(square, 1.0)
    denom = drag[:, None, None] + 16.0 / (len_x * len_y) * square[None, :, :]
    return project[None, :, :] / denom


def swap_x(stacked, sign):

    def work(piece):
        length = piece.shape[2]
        index = lax.iota(jnp.int32, length)
        cosine, sine_tab = tables(index, index, length)
        first = piece[0]
        if piece.shape[0] == 2:
            second = piece[1]
            real_part = jnp.einsum(
                "kx,zxq->zkq", cosine, first, precision=HIGH
            ) - sign * jnp.einsum("kx,zxq->zkq", sine_tab, second, precision=HIGH)
            imag_part = sign * jnp.einsum(
                "kx,zxq->zkq", sine_tab, first, precision=HIGH
            ) + jnp.einsum("kx,zxq->zkq", cosine, second, precision=HIGH)
        else:
            real_part = jnp.einsum("kx,zxq->zkq", cosine, first, precision=HIGH)
            imag_part = sign * jnp.einsum("kx,zxq->zkq", sine_tab, first, precision=HIGH)
        outgoing = jnp.stack([real_part, imag_part], 0)
        return lax.all_to_all(outgoing, "gx", split_axis=2, concat_axis=3, tiled=True)

    return work(lax.all_to_all(stacked, "gx", split_axis=3, concat_axis=2, tiled=True))


def swap_y(stacked, sign, keep_imag):

    def work(piece):
        length = piece.shape[3]
        index = lax.iota(jnp.int32, length)
        cosine, sine_tab = tables(index, index, length)
        first = piece[0]
        second = piece[1]
        real_part = jnp.einsum("ky,zpy->zpk", cosine, first, precision=HIGH) - sign * jnp.einsum(
            "ky,zpy->zpk", sine_tab, second, precision=HIGH
        )
        if keep_imag:
            imag_part = sign * jnp.einsum(
                "ky,zpy->zpk", sine_tab, first, precision=HIGH
            ) + jnp.einsum("ky,zpy->zpk", cosine, second, precision=HIGH)
            outgoing = jnp.stack([real_part, imag_part], 0)
        else:
            outgoing = real_part[None]
        return lax.all_to_all(outgoing, "gy", split_axis=3, concat_axis=2, tiled=True)

    return work(lax.all_to_all(stacked, "gy", split_axis=2, concat_axis=3, tiled=True))


def on_device(force, drag):
    planes, width_x, width_y = force.shape
    len_x = width_x * lax.axis_size("gx")
    len_y = width_y * lax.axis_size("gy")
    x_pos = lax.axis_index("gx") * width_x + lax.iota(jnp.int32, width_x)
    y_pos = lax.axis_index("gy") * width_y + lax.iota(jnp.int32, width_y)
    spectrum = swap_x(force[None], -1.0)
    green = green_block(drag, x_pos, y_pos, len_x, len_y)
    spectrum = swap_y(spectrum, -1.0, True)
    scaled = spectrum * green[None]
    inverse = swap_x(scaled, 1.0)
    inverse = swap_y(inverse, 1.0, False)
    result = inverse[0] * (1.0 / (len_x * len_y))
    return result


def solution(mesh):
    placed = (P(None, "gx", "gy"), P())
    return jax.shard_map(
        on_device, mesh=mesh, in_specs=placed, out_specs=P(None, "gx", "gy"), check_vma=False
    )
```

profile of v0, /device:TPU:0, one launch (start us, length us, event | category | flops | bytes accessed | tf_op | source)
XLA Modules:
  0.0 2023.3 jit_solution(5226011439473576461)
XLA Ops:
  5.4 100.5 %all_to_all.123 = f32[1,32,128,256]{2,1,0,3:T(8,128)S(1)} all-to-all(f32[1,32,128,256]{2,1,0,3:T(8,128)} %bitcast.140), channel_id=1, replica_groups=mesh['gx'=8,'gy'=4] {'gx'}, dimensions={3} | all-to-all | bytes 8388608 | tf_op jit(solution)/shard_map/all_to_all | solution.py:47
  108.3 5.8 copy.42
  119.0 31.7 %fusion.44 = f32[1024,1024]{0,1:S(1)} fusion(f32[1024,1024]{0,1:T(8,128)} %bitcast.141), kind=kOutput, calls=%fused_computation.44 | convolution fusion | flops 12899581952 | bytes 8388608
  150.7 30.6 %fusion.37 = f32[1024,1024]{0,1:S(1)} fusion(f32[1024,1024]{0,1:T(8,128)S(1)} %bitcast.142), kind=kOutput, calls=%fused_computation.43 | convolution fusion | flops 12899581952 | bytes 8388608
  185.9 26.4 %copy.43 = f32[2,32,1024,32]{3,1,0,2:T(8,128)} copy(f32[2,32,1024,32]{2,3,1,0:T(8,128)} %pad_maximum_fusion) | data formatting | bytes 16777216 | tf_op jit(solution)/shard_map/stack | solution.py:44
  212.3 20.5 %reshape.117 = f32[8,1,262144]{2,1,0:T(1,128)} reshape(f32[1024,2,32,32]{3,2,1,0:T(8,128)} %bitcast.125) | data formatting | bytes 16777216
  232.8 188.3 %all_to_all.124 = f32[8,1,262144]{2,1,0:T(1,128)} all-to-all(f32[8,1,262144]{2,1,0:T(1,128)} %reshape.117), channel_id=1, replica_groups=mesh['gx'=8,'gy'=4] {'gx'}, dimensions={0} | all-to-all | bytes 16777216 | tf_op jit(solution)/shard_map/all_to_all | solution.py:45
  421.7 26.4 %reduce = f32[8,262144]{1,0:T(8,128)} reduce(f32[8,1,262144]{2,1,0:T(1,128)} %all_to_all.124, f32[]{:T(128)} %broadcast.220), dimensions={1}, to_apply=%all_to_all.93.reduce_sub_computation | reduce | bytes 16777220 | tf_op jit(solution)/shard_map/all_to_all | solution.py:45
  448.1 25.3 %reshape.118 = f32[1024,2,32,32]{3,2,1,0:T(8,128)} reshape(f32[8,262144]{1,0:T(8,128)} %reduce) | data formatting | bytes 16777216
  473.3 21.8 %copy.45 = f32[2,32,128,8,32]{2,4,3,1,0:T(8,128)} copy(f32[2,32,128,8,32]{4,1,0,2,3:T(8,128)} %bitcast.126) | data formatting | bytes 16777216 | tf_op jit(solution)/shard_map/all_to_all | solution.py:45
  495.1 10.5 copy.46
  505.7 97.2 %all_to_all.125 = f32[2,32,128,256]{3,1,0,2:T(8,128)S(1)} all-to-all(f32[2,32,128,256]{3,1,0,2:T(8,128)} %copy.46), channel_id=1, replica_groups=mesh['gx'=8,'gy'=4] {'gy'}, dimensions={2} | all-to-all | bytes 16777216 | tf_op jit(solution)/shard_map/all_to_all | solution.py:70
  622.4 32.8 %fusion.21 = f32[32,32,1024]{2,1,0:T(8,128)} fusion(f32[32,32,1024]{2,1,0:T(8,128)} %squeeze.23), kind=kOutput, calls=%fused_computation.29 | convolution fusion | flops 12899581952 | bytes 8388608 | tf_op jit(solution)/shard_map/ky,zpy->zpk/dot_general | solution.py:58
  660.8 5.8 squeeze.24
  666.6 32.3 %fusion.19 = f32[32,32,1024]{2,1,0:T(8,128)S(1)} fusion(f32[32,32,1024]{2,1,0:T(8,128)} %squeeze.24), kind=kOutput, calls=%fused_computation.27 | convolution fusion | flops 12899581952 | bytes 8388608 | tf_op jit(solution)/shard_map/ky,zpy->zpk/dot_general | solution.py:64
  698.9 31.3 %subtract_bitcast_fusion.2 = f32[1,32,32,1024]{3,2,1,0:T(8,128)S(1)} fusion(f32[32,32,1024]{2,1,0:T(8,128)S(1)} %copy-done.10, f32[32,32,1024]{2,1,0:T(8,128)S(1)} %copy-done.5), kind=kOutput, calls=%fused_computation.36 | convolution fusion | flops 12901679104 | bytes 12582912 | tf_op jit(solution)/shard_map/ky,zpy->zpk/dot_general | solution.py:58
  730.2 31.7 %add_bitcast_fusion.1 = f32[1,32,32,1024]{3,2,1,0:T(8,128)S(1)} fusion(f32[32,32,1024]{2,1,0:T(8,128)S(1)} %fusion.19, f32[32,32,1024]{2,1,0:T(8,128)S(1)} %copy-done.3), kind=kOutput, calls=%fused_computation.35 | convolution fusion | flops 12901679104 | bytes 12582912 | tf_op jit(solution)/shard_map/ky,zpy->zpk/dot_general | solution.py:62
  765.9 26.4 %copy.50 = f32[2,32,32,1024]{2,1,0,3:T(8,128)} copy(f32[2,32,32,1024]{3,2,1,0:T(8,128)} %pad_maximum_fusion.1) | data formatting | bytes 16777216 | tf_op jit(solution)/shard_map/stack | solution.py:65
  792.3 33.6 %reshape.119 = f32[4,1,524288]{2,1,0:T(1,128)} reshape(f32[1024,2,32,32]{3,2,1,0:T(8,128)} %bitcast.127) | data formatting | bytes 16777216
  834.5 90.4 %all-to-all-done.3 = f32[4,1,524288]{2,1,0:T(1,128)} async-done(((f32[4,1,524288]{2,1,0:T(1,128)}), f32[4,1,524288]{2,1,0:T(1,128)}, u32[]{:S(2)}, u32[]{:S(2)}) %all-to-all-start.3) | async-done | bytes 8388640 | tf_op jit(solution)/shard_map/all_to_all | solution.py:68
  924.9 28.4 %reduce.1 = f32[4,524288]{1,0:T(4,128)} reduce(f32[4,1,524288]{2,1,0:T(1,128)} %all-to-all-done.3, f32[]{:T(128)} %broadcast.220), dimensions={1}, to_apply=%all_to_all.100.reduce_sub_computation | reduce | bytes 16777220 | tf_op jit(solution)/shard_map/all_to_all | solution.py:68
  953.3 31.1 %reshape.120 = f32[1024,2,32,32]{3,2,1,0:T(8,128)} reshape(f32[4,524288]{1,0:T(4,128)} %reduce.1) | data formatting | bytes 16777216
  984.4 22.1 %copy.68 = f32[2,32,32,4,256]{4,3,2,1,0:T(4,128)} copy(f32[2,32,32,4,256]{2,1,0,4,3:T(8,128)} %bitcast.128) | data formatting | bytes 16777216 | tf_op jit(solution)/shard_map/all_to_all | solution.py:68
  1011.8 7.6 bitcast_multiply_fusion
  1019.4 10.3 copy.53
  1029.7 187.1 %all_to_all.126 = f32[2,32,128,256]{2,1,0,3:T(8,128)S(1)} all-to-all(f32[2,32,128,256]{2,1,0,3:T(8,128)} %copy.53), channel_id=1, replica_groups=mesh['gx'=8,'gy'=4] {'gx'}, dimensions={3} | all-to-all | bytes 16777216 | tf_op jit(solution)/shard_map/all_to_all | solution.py:47
  1235.6 33.0 %fusion.7 = f32[32,32,1024]{2,1,0:T(8,128)} fusion(f32[32,1024,32]{1,2,0:T(8,128)} %squeeze.26), kind=kOutput, calls=%fused_computation.15 | convolution fusion | flops 12899581952 | bytes 8388608 | tf_op jit(solution)/shard_map/kx,zxq->zkq/dot_general | solution.py:37
  1268.6 5.8 copy.55
  1279.3 32.7 %fusion.5 = f32[32,32,1024]{2,1,0:T(8,128)S(1)} fusion(f32[32,1024,32]{1,2,0:T(8,128)} %squeeze.25), kind=kOutput, calls=%fused_computation.13 | convolution fusion | flops 12899581952 | bytes 8388608 | tf_op jit(solution)/shard_map/kx,zxq->zkq/dot_general | solution.py:38
  1312.0 31.1 %subtract_bitcast_fusion.1 = f32[1,32,1024,32]{2,3,1,0:T(8,128)S(1)} fusion(f32[32,32,1024]{2,1,0:T(8,128)S(1)} %copy-done.9, f32[32,1024,32]{1,2,0:T(8,128)S(1)} %copy-done.6), kind=kOutput, calls=%fused_computation.33 | convolution fusion | flops 12900630528 | bytes 12582912 | tf_op jit(solution)/shard_map/kx,zxq->zkq/dot_general | solution.py:35
  1343.2 31.1 %add_bitcast_fusion = f32[1,32,1024,32]{2,3,1,0:T(8,128)S(1)} fusion(f32[32,32,1024]{2,1,0:T(8,128)S(1)} %fusion.5, f32[32,1024,32]{1,2,0:T(8,128)S(1)} %copy-done.4), kind=kOutput, calls=%fused_computation.32 | convolution fusion | flops 12900630528 | bytes 12582912 | tf_op jit(solution)/shard_map/kx,zxq->zkq/dot_general | solution.py:40
  1378.4 26.4 %copy.57 = f32[2,32,1024,32]{3,1,0,2:T(8,128)} copy(f32[2,32,1024,32]{2,3,1,0:T(8,128)} %pad_maximum_fusion.2) | data formatting | bytes 16777216 | tf_op jit(solution)/shard_map/stack | solution.py:44
  1404.8 20.5 %reshape.121 = f32[8,1,262144]{2,1,0:T(1,128)} reshape(f32[1024,2,32,32]{3,2,1,0:T(8,128)} %bitcast.129) | data formatting | bytes 16777216
  1425.3 188.3 %all_to_all.127 = f32[8,1,262144]{2,1,0:T(1,128)} all-to-all(f32[8,1,262144]{2,1,0:T(1,128)} %reshape.121), channel_id=1, replica_groups=mesh['gx'=8,'gy'=4] {'gx'}, dimensions={0} | all-to-all | bytes 16777216 | tf_op jit(solution)/shard_map/all_to_all | solution.py:45
  1613.6 26.4 %reduce.2 = f32[8,262144]{1,0:T(8,128)} reduce(f32[8,1,262144]{2,1,0:T(1,128)} %all_to_all.127, f32[]{:T(128)} %broadcast.220), dimensions={1}, to_apply=%all_to_all.107.reduce_sub_computation | reduce | bytes 16777220 | tf_op jit(solution)/shard_map/all_to_all | solution.py:45
  1640.0 25.3 %reshape.122 = f32[1024,2,32,32]{3,2,1,0:T(8,128)} reshape(f32[8,262144]{1,0:T(8,128)} %reduce.2) | data formatting | bytes 16777216
  1665.2 21.8 %copy.59 = f32[2,32,128,8,32]{2,4,3,1,0:T(8,128)} copy(f32[2,32,128,8,32]{4,1,0,2,3:T(8,128)} %bitcast.130) | data formatting | bytes 16777216 | tf_op jit(solution)/shard_map/all_to_all | solution.py:45
  1687.0 10.5 copy.60
  1697.6 97.2 %all_to_all.128 = f32[2,32,128,256]{3,1,0,2:T(8,128)S(1)} all-to-all(f32[2,32,128,256]{3,1,0,2:T(8,128)} %copy.60), channel_id=1, replica_groups=mesh['gx'=8,'gy'=4] {'gy'}, dimensions={2} | all-to-all | bytes 16777216 | tf_op jit(solution)/shard_map/all_to_all | solution.py:70
  1814.3 33.0 %fusion.3 = f32[32,32,1024]{2,1,0:T(8,128)} fusion(f32[32,32,1024]{2,1,0:T(8,128)} %squeeze.28), kind=kOutput, calls=%fused_computation.11 | convolution fusion | flops 12899581952 | bytes 8388608 | tf_op jit(solution)/shard_map/ky,zpy->zpk/dot_general | solution.py:58
  1858.6 32.5 %subtract_bitcast_fusion = f32[1,32,32,1024]{3,2,1,0:T(8,128)} fusion(f32[32,32,1024]{2,1,0:T(8,128)} %fusion.3, f32[32,32,1024]{2,1,0:T(8,128)} %squeeze.27), kind=kOutput, calls=%fused_computation.31 | convolution fusion | flops 12900630528 | bytes 12582912 | tf_op jit(solution)/shard_map/ky,zpy->zpk/dot_general | solution.py:58
  1891.2 14.3 copy.64
  1905.5 11.4 reshape.123
  1916.9 54.1 %all_to_all.129 = f32[4,1,262144]{2,1,0:T(1,128)} all-to-all(f32[4,1,262144]{2,1,0:T(1,128)} %reshape.123), channel_id=1, replica_groups=mesh['gx'=8,'gy'=4] {'gy'}, dimensions={0} | all-to-all | bytes 8388608 | tf_op jit(solution)/shard_map/all_to_all | solution.py:68
  1971.0 15.3 reduce.3
  1986.3 13.7 reshape.124
  2000.0 11.7 broadcast_multiply_fusion
  2011.6 11.4 copy.65
  (52 shorter events, 119.5 us)
Async XLA Ops:
  119.0 31.7 %copy-start.7 = (f32[32,1024,32]{1,2,0:T(8,128)S(1)}, f32[32,1024,32]{1,2,0:T(8,128)}, u32[]{:S(2)}) copy-start(f32[32,1024,32]{1,2,0:T(8,128)} %squeeze.22) | copy-start | bytes 12582916
  622.4 32.8 %copy-start.1 = (f32[1,32,32,4,256]{4,2,3,1,0:T(8,128)S(1)}, f32[1,32,32,4,256]{4,2,3,1,0:T(8,128)}, u32[]{:S(2)}) copy-start(f32[1,32,32,4,256]{4,2,3,1,0:T(8,128)} %get-tuple-element.10) | copy-start | bytes 12582916
  666.5 32.3 %copy-start.5 = (f32[32,32,1024]{2,1,0:T(8,128)S(1)}, f32[32,32,1024]{2,1,0:T(8,128)}, u32[]{:S(2)}) copy-start(f32[32,32,1024]{2,1,0:T(8,128)} %squeeze.24) | copy-start | bytes 12582916
  666.6 32.4 %copy-start.10 = (f32[32,32,1024]{2,1,0:T(8,128)S(1)}, f32[32,32,1024]{2,1,0:T(8,128)}, u32[]{:S(2)}) copy-start(f32[32,32,1024]{2,1,0:T(8,128)} %fusion.21) | copy-start | bytes 12582916
  698.9 31.3 %copy-start.3 = (f32[32,32,1024]{2,1,0:T(8,128)S(1)}, f32[32,32,1024]{2,1,0:T(8,128)}, u32[]{:S(2)}) copy-start(f32[32,32,1024]{2,1,0:T(8,128)} %squeeze.23) | copy-start | bytes 12582916
  826.0 5.9 copy-start.8
  826.0 99.0 %all-to-all-start.3 = ((f32[4,1,524288]{2,1,0:T(1,128)}), f32[4,1,524288]{2,1,0:T(1,128)}, u32[]{:S(2)}, u32[]{:S(2)}) async-start(f32[4,1,524288]{2,1,0:T(1,128)} %reshape.119), calls=%async_computation.3 | async-start | bytes 16777216 | tf_op jit(solution)/shard_map/all_to_all | solution.py:68
  1235.6 33.0 %copy-start.2 = (f32[1,32,8,128,32]{3,4,2,1,0:T(8,128)S(1)}, f32[1,32,8,128,32]{3,4,2,1,0:T(8,128)}, u32[]{:S(2)}) copy-start(f32[1,32,8,128,32]{3,4,2,1,0:T(8,128)} %get-tuple-element.8) | copy-start | bytes 12582916
  1279.3 32.7 %copy-start.6 = (f32[32,1024,32]{1,2,0:T(8,128)S(1)}, f32[32,1024,32]{1,2,0:T(8,128)}, u32[]{:S(2)}) copy-start(f32[32,1024,32]{1,2,0:T(8,128)} %squeeze.25) | copy-start | bytes 12582916
  1279.3 32.7 %copy-start.9 = (f32[32,32,1024]{2,1,0:T(8,128)S(1)}, f32[32,32,1024]{2,1,0:T(8,128)}, u32[]{:S(2)}) copy-start(f32[32,32,1024]{2,1,0:T(8,128)} %fusion.7) | copy-start | bytes 12582916
  1312.0 31.1 %copy-start.4 = (f32[32,1024,32]{1,2,0:T(8,128)S(1)}, f32[32,1024,32]{1,2,0:T(8,128)}, u32[]{:S(2)}) copy-start(f32[32,1024,32]{1,2,0:T(8,128)} %squeeze.26) | copy-start | bytes 12582916
  1814.3 33.0 %copy-start = (f32[1,32,32,4,256]{4,2,3,1,0:T(8,128)S(1)}, f32[1,32,32,4,256]{4,2,3,1,0:T(8,128)}, u32[]{:S(2)}) copy-start(f32[1,32,32,4,256]{4,2,3,1,0:T(8,128)} %get-tuple-element.5) | copy-start | bytes 12582916
where the time goes:
time: 2030 us; the launch traced here: 2020 us
  blocking collectives  913 us (45%)
  local copies, waits for them, and re-layouts  499 us (25%)
  matrix products  384 us (19%)
  other arithmetic  131 us (6%)
  waiting for transfers between devices  90.4 us (4%)
    all_to_all x2, blocking collectives, work(): lax.all_to_all(outgoing, 'gx', split_axis=2, concat_axis=3, tiled=True)  377 us
    all_to_all x2, blocking collectives, swap_x(): lax.all_to_all(stacked, 'gx', split_axis=3, concat_axis=2, tiled=True)  288 us
    all_to_all x2, blocking collectives, swap_y(): lax.all_to_all(stacked, 'gy', split_axis=2, concat_axis=3, tiled=True)  194 us
    unnamed x31, local copies, waits for them, and re-layouts  187 us
    all_to_all x1, waiting for transfers between devices, work(): lax.all_to_all(outgoing, 'gy', split_axis=3, concat_axis=2, tiled=True)  90.4 us
    another operation x3, local copies, waits for them, and re-layouts, work(): outgoing = jnp.stack([real_part, imag_part], 0)  79.3 us
    dot_general x2, matrix products, work(): jnp.einsum('ky,zpy->zpk', cosine, first, precision=HIGH)  65.3 us
    all_to_all x5, local copies, waits for them, and re-layouts, work(): lax.all_to_all(outgoing, 'gx', split_axis=2, concat_axis=3, tiled=True)  65.2 us
  transfers between devices with their start and end apart: 1, of which 1 were waited for; matrix products, arithmetic and copies ran while one was open for 0% of the time, Pallas kernels for 0%

commit v1 on v0

--- a/solution.py
+++ b/solution.py
@@ -1,11 +1,240 @@
+import functools
 import math
 
 import jax
 import jax.numpy as jnp
+import numpy as np
 from jax import lax
+from jax.experimental import pallas as pl
+from jax.experimental.pallas import tpu as pltpu
 from jax.sharding import PartitionSpec as P
 
 HIGH = lax.Precision.HIGHEST
+MESH = pl.DeviceIdType.MESH
+CHUNKS = 4
+TILE = 256
+
+
+def real_modes(length):
+    half = length // 2
+    row = np.arange(length)
+    mode = np.where(row <= half, row, row - half)
+    phase = np.outer(mode, np.arange(length)) % length
+    angle = phase * (2.0 * np.pi / length)
+    table = np.where((row <= half)[:, None], np.cos(angle), np.sin(angle))
+    weight = np.where((row == 0) | (row == half), 1.0, 2.0) / length
+    return table * np.sqrt(weight)[:, None]
+
+
+def two_parts(table):
+    high = table.astype(jnp.bfloat16)
+    low = (table - high.astype(np.float64)).astype(jnp.bfloat16)
+    return high, low
+
+
+def split(value):
+    high = value.astype(jnp.bfloat16)
+    return high, (value - high.astype(jnp.float32)).astype(jnp.bfloat16)
+
+
+def product(a_high, a_low, b_high, b_low):
+    dot = functools.partial(jnp.dot, preferred_element_type=jnp.float32)
+    return dot(a_high, b_high) + (dot(a_high, b_low) + dot(a_low, b_high))
+
+
+def plane_kernel(
+    nx, ny, force, drag, tables_in, turned_in, out, plane, green, table, turned, part, lines, modes,
+    table_sem, send, recv, back_send, back_recv,
+):
+    gx, gy = lax.axis_index("gx"), lax.axis_index("gy")
+    me = gx * ny + gy
+    devices = nx * ny
+    chunks, rows = plane.shape[1], plane.shape[2]
+    width = force.shape[2]
+    length = plane.shape[3]
+    len_x = nx * chunks * rows
+    count = nx * rows
+
+    def peer(i):
+        px = lax.rem(gx + (nx - 1 - lax.rem(i, nx)), nx)
+        py = lax.rem(gy + (ny - 1 - i // nx), ny)
+        return px, py
+
+    def columns(j, size):
+        return pl.ds(pl.multiple_of(j * size, size), size)
+
+    def band(c):
+        return pl.ds(pl.multiple_of(c * rows, rows), rows)
+
+    loads = [
+        pltpu.make_async_copy(tables_in, table, table_sem.at[0]),
+        pltpu.make_async_copy(turned_in, turned, table_sem.at[1]),
+    ]
+    for load in loads:
+        load.start()
+
+    barrier = pltpu.get_barrier_semaphore()
+
+    @pl.loop(0, devices - 1)
+    def _(i):
+        pl.semaphore_signal(barrier, inc=1, device_id=peer(i), device_id_type=MESH)
+
+    pl.semaphore_wait(barrier, devices - 1)
+
+    @pl.loop(0, chunks)
+    def _(c):
+        @pl.loop(0, devices - 1)
+        def _(i):
+            px, py = peer(i)
+            pltpu.make_async_remote_copy(
+                src_ref=force.at[px * ny + py, band(c)],
+                dst_ref=plane.at[gx, c, :, columns(gy, width)],
+                send_sem=send.at[c],
+                recv_sem=recv.at[c],
+                device_id=(px, py),
+                device_id_type=MESH,
+            ).start()
+
+        pltpu.make_async_copy(
+            force.at[me, band(c)], plane.at[gx, c, :, columns(gy, width)], recv.at[c]
+        ).start()
+
+    friction = drag[me]
+
+    @pl.loop(0, len_x // TILE)
+    def _(i):
+        first = lax.broadcasted_iota(jnp.int32, (TILE, length), 0) + i * TILE
+        second = lax.broadcasted_iota(jnp.int32, (TILE, length), 1)
+        mode_x = jnp.where(first <= len_x // 2, first, first - len_x // 2).astype(jnp.float32)
+        mode_y = jnp.where(second <= length // 2, second, second - length // 2).astype(jnp.float32)
+        square_x = mode_x * mode_x
+        square = square_x + mode_y * mode_y
+        floor = jnp.maximum(square, 1.0)
+        denom = friction + 16.0 / (len_x * length) * square
+        green[columns(i, TILE), :] = (floor - square_x) / (floor * denom)
+
+    for load in loads:
+        load.wait()
+
+    @pl.loop(0, chunks)
+    def _(c):
+        pltpu.make_async_copy(plane.at[:, c], plane.at[:, c], recv.at[c]).wait()
+        high, low = split(plane[:, c].reshape(count, length))
+        part[0] = high
+        part[1] = low
+
+        @pl.loop(0, length // TILE)
+        def _(j):
+            cols = columns(j, TILE)
+            result = product(
+                part[0],
+                part[1],
+                turned[0, :, :, :, cols].reshape(length, TILE),
+                turned[1, :, :, :, cols].reshape(length, TILE),
+            )
+            high, low = split(result)
+            lines[0, :, c, :, cols] = high.reshape(nx, rows, TILE)
+            lines[1, :, c, :, cols] = low.reshape(nx, rows, TILE)
+
+    @pl.loop(0, length // TILE)
+    def _(j):
+        cols = columns(j, TILE)
+
+        @pl.loop(0, len_x // (2 * TILE))
+        def _(i):
+            band_i = columns(i, 2 * TILE)
+            result = product(
+                table[0, band_i, :],
+                table[1, band_i, :],
+                lines[0, :, :, :, cols].reshape(len_x, TILE),
+                lines[1, :, :, :, cols].reshape(len_x, TILE),
+            )
+            high, low = split(result * green[band_i, cols])
+            modes[0, band_i, cols] = high
+            modes[1, band_i, cols] = low
+
+    @pl.loop(0, chunks)
+    def _(c):
+        @pl.loop(0, length // TILE)
+        def _(j):
+            cols = columns(j, TILE)
+            result = product(
+                turned[0, :, c].reshape(count, len_x),
+                turned[1, :, c].reshape(count, len_x),
+                modes[0, :, cols],
+                modes[1, :, cols],
+            )
+            high, low = split(result)
+            part[0, :, cols] = high
+            part[1, :, cols] = low
+
+        @pl.loop(0, length // TILE)
+        def _(j):
+            cols = columns(j, TILE)
+            result = product(part[0], part[1], table[0, :, cols], table[1, :, cols])
+            plane[:, c, :, cols] = result.reshape(nx, rows, TILE)
+
+        @pl.loop(0, devices - 1)
+        def _(i):
+            px, py = peer(i)
+            pltpu.make_async_remote_copy(
+                src_ref=plane.at[px, c, :, columns(py, width)],
+                dst_ref=out.at[me, band(c)],
+                send_sem=back_send.at[c],
+                recv_sem=back_recv.at[c],
+                device_id=(px, py),
+                device_id_type=MESH,
+            ).start()
+
+        pltpu.make_async_copy(
+            plane.at[gx, c, :, columns(gy, width)], out.at[me, band(c)], back_recv.at[c]
+        ).start()
+
+    @pl.loop(0, chunks)
+    def _(c):
+        sent = force.at[pl.ds(0, devices - 1), band(c)]
+        pltpu.make_async_copy(sent, sent, send.at[c]).wait()
+        pltpu.make_async_copy(sent, sent, back_send.at[c]).wait()
+        landed = out.at[:, band(c)]
+        pltpu.make_async_copy(landed, landed, back_recv.at[c]).wait()
+
+
+def by_planes(force, drag):
+    nx, ny = lax.axis_size("gx"), lax.axis_size("gy")
+    planes, width_x, width_y = force.shape
+    length = width_x * nx
+    rows = width_x // CHUNKS
+    modes = real_modes(length)
+    table = np.stack(two_parts(modes))
+    turned = np.stack(two_parts(modes.T)).reshape(2, nx, CHUNKS, rows, length)
+    anywhere = pl.BlockSpec(memory_space=pl.ANY)
+    bf16, f32 = jnp.bfloat16, jnp.float32
+    return pl.pallas_call(
+        functools.partial(plane_kernel, nx, ny),
+        out_shape=jax.ShapeDtypeStruct(force.shape, force.dtype),
+        in_specs=[anywhere, pl.BlockSpec(memory_space=pltpu.SMEM), anywhere, anywhere],
+        out_specs=anywhere,
+        scratch_shapes=[
+            pltpu.VMEM((nx, CHUNKS, rows, length), f32),
+            pltpu.VMEM((length, length), f32),
+            pltpu.VMEM((2, length, length), bf16),
+            pltpu.VMEM((2, nx, CHUNKS, rows, length), bf16),
+            pltpu.VMEM((2, nx * rows, length), bf16),
+            pltpu.VMEM((2, nx, CHUNKS, rows, length), bf16),
+            pltpu.VMEM((2, length, length), bf16),
+            pltpu.SemaphoreType.DMA((2,)),
+            pltpu.SemaphoreType.DMA((CHUNKS,)),
+            pltpu.SemaphoreType.DMA((CHUNKS,)),
+            pltpu.SemaphoreType.DMA((CHUNKS,)),
+            pltpu.SemaphoreType.DMA((CHUNKS,)),
+        ],
+        compiler_params=pltpu.CompilerParams(
+            collective_id=0, has_side_effects=True, vmem_limit_bytes=48 * 1024 * 1024
+        ),
+        cost_estimate=pl.CostEstimate(
+            flops=24 * length**3, bytes_accessed=8 * force.size, transcendentals=0
+        ),
+    )(force, drag, jnp.asarray(table), jnp.asarray(turned))
 
 
 def tables(row_pos, col_pos, length):
@@ -74,6 +303,9 @@
     planes, width_x, width_y = force.shape
     len_x = width_x * lax.axis_size("gx")
     len_y = width_y * lax.axis_size("gy")
+    whole_planes = planes == lax.axis_size("gx") * lax.axis_size("gy") and len_x == len_y
+    if whole_planes and width_x % (16 * CHUNKS) == 0 and width_y % TILE == 0:
+        return by_planes(force, drag)
     x_pos = lax.axis_index("gx") * width_x + lax.iota(jnp.int32, width_x)
     y_pos = lax.axis_index("gy") * width_y + lax.iota(jnp.int32, width_y)
     spectrum = swap_x(force[None], -1.0)

time: 2030 us -> 209 us (0.10)
  blocking collectives: 913 us -> 0 us
  local copies, waits for them, and re-layouts: 499 us -> 2.67 us
  matrix products: 384 us -> 0 us
  Pallas kernels: 0 us -> 207 us
  other arithmetic: 131 us -> 0 us
  waiting for transfers between devices: 90.4 us -> 0 us
    all_to_all x7 -> x0, blocking collectives: 913 us -> none  [the longest x2 377 us: work(): lax.all_to_all(outgoing, 'gx', split_axis=2, concat_axis=3, tiled=True)]
    dot_general x10 -> x0, matrix products: 321 us -> none  [the longest x2 65.3 us: work(): jnp.einsum('ky,zpy->zpk', cosine, first, precision=HIGH)]
    pallas_call x0 -> x1, Pallas kernels: none -> 207 us  [by_planes(): pl.pallas_call(functools.partial(plane_kernel, nx, ny), out_shape=jax.Sha...]
    unnamed x31 -> x3, local copies, waits for them, and re-layouts: 187 us -> 2.67 us
    all_to_all x12 -> x0, local copies, waits for them, and re-layouts: 115 us -> none  [the longest x5 65.2 us: work(): lax.all_to_all(outgoing, 'gx', split_axis=2, concat_axis=3, tiled=True)]
    all_to_all x4 -> x0, other arithmetic: 96.4 us -> none  [the longest x2 52.7 us: work(): lax.all_to_all(outgoing, 'gx', split_axis=2, concat_axis=3, tiled=True)]
    all_to_all x1 -> x0, waiting for transfers between devices: 90.4 us -> none  [work(): lax.all_to_all(outgoing, 'gy', split_axis=3, concat_axis=2, tiled=True)]
    another operation x3 -> x0, local copies, waits for them, and re-layouts: 79.3 us -> none  [work(): outgoing = jnp.stack([real_part, imag_part], 0)]
  transfers between devices with their start and end apart: 1 -> 0, of which waited for: 1 -> 0; matrix products, arithmetic and copies ran while one was open for 0% -> 0% of each run, Pallas kernels for 0% -> 0%
where the time goes in v1:
time: 209 us
  Pallas kernels  207 us (99%)
  local copies, waits for them, and re-layouts  2.67 us (1%)
    pallas_call x1, Pallas kernels, by_planes(): pl.pallas_call(functools.partial(plane_kernel, nx, ny), out_shape=jax.Sha...  207 us

profile of v1, /device:TPU:0, one launch (start us, length us, event | category | flops | bytes accessed | tf_op | source)
XLA Modules:
  0.0 209.3 jit_solution(2050583530385441343)
XLA Ops:
  0.0 0.0 copy-start
  0.0 0.7 copy-done
  0.7 206.6 %shard_map.46 = f32[32,128,256]{2,1,0:T(8,128)S(1)} custom-call(f32[32,128,256]{2,1,0:T(8,128)} %force.1, f32[32]{0:T(128)S(1)} %copy-done, bf16[2,1024,1024]{2,1,0:T(8,128)(2,1)} %constant.4.clone.tables_in, bf16[2,8,4,32,1024]{4,3,2,1,0:T(8,128)(2,1)} %constant.5.clone.turned_in), custom_call_target="tpu_custom_call" | custom-call | flops 25769803776 | bytes 8388608 | tf_op jit(solution)/shard_map/pallas_call | solution.py:212
  207.3 2.0 copy.6
Async XLA Ops:
  0.0 0.7 copy-start

commit v2 on v1

--- a/solution.py
+++ b/solution.py
@@ -11,7 +11,7 @@
 
 HIGH = lax.Precision.HIGHEST
 MESH = pl.DeviceIdType.MESH
-CHUNKS = 4
+CHUNKS = 8
 TILE = 256
 
 
@@ -43,7 +43,8 @@
 
 
 def plane_kernel(
-    nx, ny, force, drag, tables_in, turned_in, out, plane, green, table, turned, part, lines, modes,
+    nx, ny, force, drag, tables_in, turned_in, pieces_in, out, plane, green, table, turned, pieces, part, lines,
+    total, modes,
     table_sem, send, recv, back_send, back_recv,
 ):
     gx, gy = lax.axis_index("gx"), lax.axis_index("gy")
@@ -69,6 +70,7 @@
     loads = [
         pltpu.make_async_copy(tables_in, table, table_sem.at[0]),
         pltpu.make_async_copy(turned_in, turned, table_sem.at[1]),
+        pltpu.make_async_copy(pieces_in, pieces, table_sem.at[2]),
     ]
     for load in loads:
         load.start()
@@ -111,13 +113,13 @@
         square = square_x + mode_y * mode_y
         floor = jnp.maximum(square, 1.0)
         denom = friction + 16.0 / (len_x * length) * square
+        total[columns(i, TILE), :] = jnp.zeros((TILE, length), jnp.float32)
         green[columns(i, TILE), :] = (floor - square_x) / (floor * denom)
 
     for load in loads:
         load.wait()
 
-    @pl.loop(0, chunks)
-    def _(c):
+    def arrive(c, last):
         pltpu.make_async_copy(plane.at[:, c], plane.at[:, c], recv.at[c]).wait()
         high, low = split(plane[:, c].reshape(count, length))
         part[0] = high
@@ -133,25 +135,31 @@
                 turned[1, :, :, :, cols].reshape(length, TILE),
             )
             high, low = split(result)
-            lines[0, :, c, :, cols] = high.reshape(nx, rows, TILE)
-            lines[1, :, c, :, cols] = low.reshape(nx, rows, TILE)
-
-    @pl.loop(0, length // TILE)
-    def _(j):
-        cols = columns(j, TILE)
-
-        @pl.loop(0, len_x // (2 * TILE))
-        def _(i):
-            band_i = columns(i, 2 * TILE)
-            result = product(
-                table[0, band_i, :],
-                table[1, band_i, :],
-                lines[0, :, :, :, cols].reshape(len_x, TILE),
-                lines[1, :, :, :, cols].reshape(len_x, TILE),
-            )
-            high, low = split(result * green[band_i, cols])
-            modes[0, band_i, cols] = high
-            modes[1, band_i, cols] = low
+            lines[0, :, cols] = high
+            lines[1, :, cols] = low
+
+        @pl.loop(0, length // TILE)
+        def _(j):
+            cols = columns(j, TILE)
+
+            @pl.loop(0, len_x // (2 * TILE))
+            def _(i):
+                band_i = columns(i, 2 * TILE)
+                result = total[band_i, cols] + product(
+                    pieces[0, c, band_i, :], pieces[1, c, band_i, :], lines[0, :, cols], lines[1, :, cols]
+                )
+                if last:
+                    high, low = split(result * green[band_i, cols])
+                    modes[0, band_i, cols] = high
+                    modes[1, band_i, cols] = low
+                else:
+                    total[band_i, cols] = result
+
+    @pl.loop(0, chunks - 1)
+    def _(c):
+        arrive(c, False)
+
+    arrive(chunks - 1, True)
 
     @pl.loop(0, chunks)
     def _(c):
@@ -207,22 +215,25 @@
     modes = real_modes(length)
     table = np.stack(two_parts(modes))
     turned = np.stack(two_parts(modes.T)).reshape(2, nx, CHUNKS, rows, length)
+    pieces = table.reshape(2, length, nx, CHUNKS, rows).transpose(0, 3, 1, 2, 4).reshape(2, CHUNKS, length, nx * rows)
     anywhere = pl.BlockSpec(memory_space=pl.ANY)
     bf16, f32 = jnp.bfloat16, jnp.float32
     return pl.pallas_call(
         functools.partial(plane_kernel, nx, ny),
         out_shape=jax.ShapeDtypeStruct(force.shape, force.dtype),
-        in_specs=[anywhere, pl.BlockSpec(memory_space=pltpu.SMEM), anywhere, anywhere],
+        in_specs=[anywhere, pl.BlockSpec(memory_space=pltpu.SMEM), anywhere, anywhere, anywhere],
         out_specs=anywhere,
         scratch_shapes=[
             pltpu.VMEM((nx, CHUNKS, rows, length), f32),
             pltpu.VMEM((length, length), f32),
             pltpu.VMEM((2, length, length), bf16),
             pltpu.VMEM((2, nx, CHUNKS, rows, length), bf16),
+            pltpu.VMEM((2, CHUNKS, length, nx * rows), bf16),
             pltpu.VMEM((2, nx * rows, length), bf16),
-            pltpu.VMEM((2, nx, CHUNKS, rows, length), bf16),
+            pltpu.VMEM((2, nx * rows, length), bf16),
+            pltpu.VMEM((length, length), f32),
             pltpu.VMEM((2, length, length), bf16),
-            pltpu.SemaphoreType.DMA((2,)),
+            pltpu.SemaphoreType.DMA((3,)),
             pltpu.SemaphoreType.DMA((CHUNKS,)),
             pltpu.SemaphoreType.DMA((CHUNKS,)),
             pltpu.SemaphoreType.DMA((CHUNKS,)),
@@ -234,7 +245,7 @@
         cost_estimate=pl.CostEstimate(
             flops=24 * length**3, bytes_accessed=8 * force.size, transcendentals=0
         ),
-    )(force, drag, jnp.asarray(table), jnp.asarray(turned))
+    )(force, drag, jnp.asarray(table), jnp.asarray(turned), jnp.asarray(pieces))
 
 
 def tables(row_pos, col_pos, length):

time: 209 us -> 202 us (0.967)
  Pallas kernels: 207 us -> 199 us
    pallas_call x1, Pallas kernels: 207 us -> 199 us  [by_planes(): pl.pallas_call(functools.partial(plane_kernel, nx, ny), out_shape=jax.Sha...]
where the time goes in v2:
time: 202 us
  Pallas kernels  199 us (99%)
  local copies, waits for them, and re-layouts  2.67 us (1%)
    pallas_call x1, Pallas kernels, by_planes(): pl.pallas_call(functools.partial(plane_kernel, nx, ny), out_shape=jax.Sha...  199 us

profile of v2, /device:TPU:0, one launch (start us, length us, event | category | flops | bytes accessed | tf_op | source)
XLA Modules:
  0.0 202.0 jit_solution(10069431711443087771)
XLA Ops:
  0.0 0.0 copy-start
  0.0 0.7 copy-done
  0.7 199.3 %shard_map.55 = f32[32,128,256]{2,1,0:T(8,128)S(1)} custom-call(f32[32,128,256]{2,1,0:T(8,128)} %force.1, f32[32]{0:T(128)S(1)} %copy-done, bf16[2,1024,1024]{2,1,0:T(8,128)(2,1)} %constant.6.clone.tables_in, bf16[2,8,8,16,1024]{4,3,2,1,0:T(8,128)(2,1)} %constant.7.clone.turned_in, bf16[2,8,1024,128]{3,2,1,0:T(8,128)(2,1)} %constant.8.clone.pieces_in), custom_call_target="tpu_custom_call" | custom-call | flops 25769803776 | bytes 8388608 | tf_op jit(solution)/shard_map/pallas_call | solution.py:221
  200.0 2.0 copy.7
Async XLA Ops:
  0.0 0.7 copy-start

commit v3 on v2

--- a/solution.py
+++ b/solution.py
@@ -13,6 +13,7 @@
 MESH = pl.DeviceIdType.MESH
 CHUNKS = 8
 TILE = 256
+WIDE = 512
 
 
 def real_modes(length):
@@ -125,14 +126,14 @@
         part[0] = high
         part[1] = low
 
-        @pl.loop(0, length // TILE)
+        @pl.loop(0, length // WIDE)
         def _(j):
-            cols = columns(j, TILE)
+            cols = columns(j, WIDE)
             result = product(
                 part[0],
                 part[1],
-                turned[0, :, :, :, cols].reshape(length, TILE),
-                turned[1, :, :, :, cols].reshape(length, TILE),
+                turned[0, :, :, :, cols].reshape(length, WIDE),
+                turned[1, :, :, :, cols].reshape(length, WIDE),
             )
             high, low = split(result)
             lines[0, :, cols] = high
@@ -163,9 +164,9 @@
 
     @pl.loop(0, chunks)
     def _(c):
-        @pl.loop(0, length // TILE)
+        @pl.loop(0, length // WIDE)
         def _(j):
-            cols = columns(j, TILE)
+            cols = columns(j, WIDE)
             result = product(
                 turned[0, :, c].reshape(count, len_x),
                 turned[1, :, c].reshape(count, len_x),
@@ -176,11 +177,11 @@
             part[0, :, cols] = high
             part[1, :, cols] = low
 
-        @pl.loop(0, length // TILE)
+        @pl.loop(0, length // WIDE)
         def _(j):
-            cols = columns(j, TILE)
+            cols = columns(j, WIDE)
             result = product(part[0], part[1], table[0, :, cols], table[1, :, cols])
-            plane[:, c, :, cols] = result.reshape(nx, rows, TILE)
+            plane[:, c, :, cols] = result.reshape(nx, rows, WIDE)
 
         @pl.loop(0, devices - 1)
         def _(i):
@@ -315,7 +316,7 @@
     len_x = width_x * lax.axis_size("gx")
     len_y = width_y * lax.axis_size("gy")
     whole_planes = planes == lax.axis_size("gx") * lax.axis_size("gy") and len_x == len_y
-    if whole_planes and width_x % (16 * CHUNKS) == 0 and width_y % TILE == 0:
+    if whole_planes and width_x % (16 * CHUNKS) == 0 and width_y % TILE == 0 and len_y % WIDE == 0:
         return by_planes(force, drag)
     x_pos = lax.axis_index("gx") * width_x + lax.iota(jnp.int32, width_x)
     y_pos = lax.axis_index("gy") * width_y + lax.iota(jnp.int32, width_y)

time: 202 us -> 201 us (level)
  no operation moved by 1% of the time
where the time goes in v3:
time: 201 us
  Pallas kernels  198 us (99%)
  local copies, waits for them, and re-layouts  2.67 us (1%)
    pallas_call x1, Pallas kernels, by_planes(): pl.pallas_call(functools.partial(plane_kernel, nx, ny), out_shape=jax.Sha...  198 us

profile of v3, /device:TPU:0, one launch (start us, length us, event | category | flops | bytes accessed | tf_op | source)
XLA Modules:
  0.0 200.7 jit_solution(6592383535065514308)
XLA Ops:
  0.0 0.0 copy-start
  0.0 0.7 copy-done
  0.7 198.0 %shard_map.55 = f32[32,128,256]{2,1,0:T(8,128)S(1)} custom-call(f32[32,128,256]{2,1,0:T(8,128)} %force.1, f32[32]{0:T(128)S(1)} %copy-done, bf16[2,1024,1024]{2,1,0:T(8,128)(2,1)} %constant.6.clone.tables_in, bf16[2,8,8,16,1024]{4,3,2,1,0:T(8,128)(2,1)} %constant.7.clone.turned_in, bf16[2,8,1024,128]{3,2,1,0:T(8,128)(2,1)} %constant.8.clone.pieces_in), custom_call_target="tpu_custom_call" | custom-call | flops 25769803776 | bytes 8388608 | tf_op jit(solution)/shard_map/pallas_call | solution.py:222
  198.7 2.0 %copy.7 = f32[32,128,256]{2,1,0:T(8,128)} copy(f32[32,128,256]{2,1,0:T(8,128)S(1)} %shard_map.55) | data formatting | bytes 8388608
Async XLA Ops:
  0.0 0.7 copy-start
